TPU v7x, 32 devices: a whole 2x2x4 slice. The times are simulated.
32 devices in a mesh: groups: 2 (over x), space: 16 (over z, y, core).
Axes of the slice: x: 2, y: 2, z: 4, core: 2. Of those that a mesh axis runs over, the one named last changes fastest.
Arguments:
- conductivity: float32 [64, 256, 128], P('space', 'groups'), parts along dimension 1, may hold values from 0.3 to 3
- forward: float32 [16, 64, 128, 128], P('groups', 'space'), parts along dimension 0, may hold values from -6 to 6
- adjoint_rhs: float32 [16, 64, 128, 128], P('groups', 'space'), parts along dimension 0, may hold values from -6 to 6
- plane_counts: int32 [32], P('groups'), parts along dimension 0, may hold values from 1 to 4, 32 in all
Outputs:
- adjoint: float32 [16, 64, 128, 128], P('groups', 'space'), parts along dimension 0
- gradient: float32 [64, 256, 128], P('space', 'groups'), parts along dimension 1
There are 2 independent parts, one for each index of `groups`. A program takes and returns all parts, laid end to end along the dimension named above; each array names one. Nothing has to cross between parts.
Inputs may be any that keep to these rules, and one draw needn't show every extreme that they name: `plane_counts`: they sum to 32, and the largest is exactly 4.
All inputs are finite; a program needn't handle non-finite values.
Results may differ from a plain program's by a relative error of at most 0.0001.
Values sent between devices are 32-bit elements; how exact they have to be, the bound alone decides.
A program may use at most 128 MiB of HBM per device.

v0:
```python
import jax
import jax.numpy as jnp
from jax import lax
from jax.sharding import PartitionSpec as P

NU = 2
NC = 4
CYCLES = 2


OMEGA = 0.8


def extended_2(shard, sides, width):
    for axis, dim in sides:
        peers, length = (lax.axis_size(axis), shard.shape[dim])
        up = [(i, (i + 1) % peers) for i in range(peers - 1)]
        down = [(j, i) for i, j in up]
        last = lax.slice_in_dim(shard, length - width, length, axis=dim)
        leading = lax.slice_in_dim(shard, 0, width, axis=dim)
        before = lax.ppermute(last, axis, up)
        after = lax.ppermute(leading, axis, down)
        shard = jnp.concatenate([before, shard, after], axis=dim)
    return shard


def take_last(values, planes_here):
    return lax.dynamic_index_in_dim(values, planes_here - 1, 1, keepdims=False)


def slab_neighbors(values, lower_plane, upper_plane, planes_here):
    slots_here = values.shape[1]
    lower_side = jnp.concatenate([lower_plane[:, None], values[:, :-1]], axis=1)
    upper_side = jnp.concatenate([values[:, 1:], jnp.zeros_like(values[:, :1])], axis=1)
    is_top = (jnp.arange(slots_here) == planes_here - 1)[None, :, None, None]
    upper_side = jnp.where(is_top, upper_plane[:, None], upper_side)
    padded = jnp.pad(values, ((0, 0), (0, 0), (1, 1), (1, 1)))
    return [
        lower_side,
        upper_side,
        padded[:, :, :-2, 1:-1],
        padded[:, :, 2:, 1:-1],
        padded[:, :, 1:-1, :-2],
        padded[:, :, 1:-1, 2:],
    ]


def face_values(conduct, neighbor_list, x_weight):
    weights = [x_weight, x_weight, 1.0, 1.0, 1.0, 1.0]
    return [(conduct + neighbor_list[position]) * 0.5 * weights[position] for position in range(6)]


def total_of(terms_list):
    accum = terms_list[0]
    for position in range(1, len(terms_list)):
        accum = accum + terms_list[position]
    return accum


def apply_op(values, face_list, neighbor_list):
    return total_of(
        [face_list[position] * (values - neighbor_list[position]) for position in range(6)]
    )


def relax_with(values, source_term, face_list, diagonal, neighbor_list):
    image = apply_op(values, face_list, neighbor_list)
    return values + OMEGA * (source_term - image) / diagonal


def block_sum(values):
    shape = values.shape
    return values.reshape(shape[0], shape[1], shape[2] // 4, 4, shape[3] // 4, 4).sum(axis=(3, 5))


def block_mean(values):
    shape = values.shape
    return values.reshape(shape[0], shape[1], shape[2] // 4, 4, shape[3] // 4, 4).mean(axis=(3, 5))


def expand(values):
    return jnp.repeat(jnp.repeat(values, 4, axis=2), 4, axis=3)


def fine_near(values, planes_here):
    edge_planes = jnp.stack([values[:, 0], take_last(values, planes_here)], axis=1)
    extended = extended_2(edge_planes, (("space", 1),), 1)
    return slab_neighbors(values, extended[:, 0], extended[:, 3], planes_here)


def coarse_near(values, planes_here):
    edge_planes = jnp.stack([values[:, 0], take_last(values, planes_here)], axis=1)
    extended = extended_2(edge_planes, (("space", 1),), 1)
    return slab_neighbors(values, extended[:, 0], extended[:, 3], planes_here)


def shards(conductivity, forward, adjoint_rhs, plane_counts):
    slots_here = conductivity.shape[0]
    position_here = lax.axis_index("space")
    planes_here = plane_counts[position_here]
    alive_mask = (jnp.arange(slots_here) < planes_here)[None, :, None, None]
    conduct = conductivity[None]
    conduct_edges = jnp.stack(
        [
            conductivity[0],
            lax.dynamic_index_in_dim(conductivity, planes_here - 1, 0, keepdims=False),
        ],
        axis=0,
    )[None]
    forward_edges = jnp.stack([forward[:, 0], take_last(forward, planes_here)], axis=1)
    fixed_ext = extended_2(
        jnp.concatenate([conduct_edges, forward_edges], axis=0), (("space", 1),), 1
    )
    conduct_near = slab_neighbors(conduct, fixed_ext[:1, 0], fixed_ext[:1, 3], planes_here)
    forward_near = slab_neighbors(forward, fixed_ext[1:, 0], fixed_ext[1:, 3], planes_here)
    fine_faces = face_values(conduct, conduct_near, 1.0)
    fine_diag = jnp.where(alive_mask, total_of(fine_faces), 1.0)
    coarse_conduct = block_mean(conduct)
    lower_coarse = block_mean(fixed_ext[:1, 0][:, None])[:, 0]
    upper_coarse = block_mean(fixed_ext[:1, 3][:, None])[:, 0]
    coarse_faces = face_values(
        coarse_conduct,
        slab_neighbors(coarse_conduct, lower_coarse, upper_coarse, planes_here),
        16.0,
    )
    coarse_diag = jnp.where(alive_mask, total_of(coarse_faces), 1.0)

    def smooth(values, source_term):
        updated = relax_with(
            values, source_term, fine_faces, fine_diag, fine_near(values, planes_here)
        )
        return jnp.where(alive_mask, updated, 0.0)

    source_term = jnp.where(alive_mask, adjoint_rhs, 0.0)
    adjoint = jnp.zeros(source_term.shape, jnp.float32)
    for cycle_index in range(CYCLES):
        for sweep_index in range(NU):
            adjoint = smooth(adjoint, source_term)
        residue = source_term - apply_op(adjoint, fine_faces, fine_near(adjoint, planes_here))
        residue = jnp.where(alive_mask, residue, 0.0)
        coarse_res = block_sum(residue)
        correction = jnp.zeros(coarse_res.shape, jnp.float32)
        for coarse_sweep_index in range(NC):
            coarse_updated = relax_with(
                correction,
                coarse_res,
                coarse_faces,
                coarse_diag,
                coarse_near(correction, planes_here),
            )
            correction = jnp.where(alive_mask, coarse_updated, 0.0)
        adjoint = adjoint + expand(correction)
        for sweep_index in range(NU):
            adjoint = smooth(adjoint, source_term)
    adjoint_near = fine_near(adjoint, planes_here)
    products = total_of(
        [
            (forward - forward_near[position]) * (adjoint - adjoint_near[position])
            for position in range(6)
        ]
    )
    grad_field = -0.5 * jnp.sum(products, axis=0)
    grad_field = jnp.where(alive_mask[0], grad_field, 0.0)
    return (adjoint, grad_field)


def solution(mesh):
    in_specs = (
        P("space", "groups", None),
        P("groups", "space", None, None),
        P("groups", "space", None, None),
        P("groups"),
    )
    out_specs = (P("groups", "space", None, None), P("space", "groups", None))
    return jax.shard_map(shards, mesh=mesh, in_specs=in_specs, out_specs=out_specs, check_vma=False)
```

profile of v0, /device:TPU:17, one launch (start us, length us, event | category | flops | bytes accessed | tf_op | source)
XLA Modules:
  0.0 495.3 jit_solution(14760996451111808728)
XLA Ops:
  4.0 3.0 collective-permute-start.1
  15.0 3.6 collective-permute-start
  22.0 10.1 %reshape_broadcast_in_dim.3 = f32[4,32,4,32,4]{4,3,2,1,0:T(8,128)} reshape(f32[4,128,128]{2,1,0:T(8,128)S(1)} %copy-done.23) | data formatting | bytes 524288 | tf_op jit(solution)/shard_map/reshape;broadcast_in_dim | solution.py:78
  32.1 4.1 reduce_sum.55
  39.7 3.1 collective-permute-start.8
  51.8 4.0 fusion.312
  58.1 3.4 collective-permute-start.5
  63.7 3.5 reshape_broadcast_in_dim_squeeze.6
  69.6 3.5 reshape_broadcast_in_dim_squeeze.7
  79.7 3.9 fusion.325
  83.8 4.4 collective-permute-start.7
  91.3 3.9 collective-permute-done.7
  95.2 6.8 %collective-permute-done.6 = f32[8,1,128,128]{2,0,3,1:T(8,128)S(1)} collective-permute-done((f32[8,1,128,128]{2,0,3,1:T(8,128)S(1)}, f32[8,1,128,128]{2,0,3,1:T(8,128)S(1)}, u32[]{:S(2)}, u32[]{:S(2)}) %collective-permute-start.6) | collective-permute-done | bytes 524320 | tf_op jit(solution)/shard_map/ppermute | solution.py:21
  102.0 3.7 fusion.131
  105.7 26.3 %copy.144 = f32[8,4,128,128]{0,3,2,1:T(8,128)} copy(f32[8,4,128,128]{2,0,3,1:T(8,128)} %fusion.131) | data formatting | bytes 4194304 | tf_op jit(solution)/shard_map/jit(_where)/select_n | solution.py:140
  131.9 14.4 %reduce_sum.54 = f32[8,4,32,32]{0,3,2,1:T(8,128)} reduce(f32[8,4,32,4,32,4]{0,5,4,3,2,1:T(4,128)} %bitcast.90, f32[]{:T(128)} %constant.82.clone.1), dimensions={3,5}, to_apply=%region_0.1 | reduce | flops 491520 | bytes 2228228 | tf_op jit(solution)/shard_map/reduce_sum | solution.py:73
  148.0 6.2 %divide_select_fusion.1 = f32[8,4,32,32]{0,3,2,1:T(8,128)S(1)} fusion(f32[8,4,32,32]{0,3,2,1:T(8,128)S(1)} %copy-done.7, f32[4,32,32]{2,1,0:T(8,128)S(1)} %get-tuple-element.98, pred[4]{0:T(512)(128)(4,1)S(1)} %iota_compare_fusion.1, f32[8,4,32,32]{0,3,2,1:T(8,128)S(1)} %broadcast.194, f32[4,32,32]{2,1,0:T(8,128)} %get-tuple-element.102, ...), kind=kLoop, calls=%fused_computation.406 | loop fusion | flops 720896 | bytes 573448 | tf_op jit(solution)/shard_map/jit(_where)/select_n | solution.py:151
  156.5 4.3 collective-permute-start.10
  161.2 9.9 %collective-permute-done.11 = f32[8,1,32,32]{0,3,2,1:T(8,128)S(1)} collective-permute-done((f32[8,1,32,32]{0,3,2,1:T(8,128)S(1)}, f32[8,1,32,32]{0,3,2,1:T(8,128)S(1)}, u32[]{:S(2)}, u32[]{:S(2)}) %collective-permute-start.11) | collective-permute-done | bytes 32800 | tf_op jit(solution)/shard_map/ppermute | solution.py:22
  171.1 4.5 fusion.318
  177.6 3.6 collective-permute-start.12
  181.8 10.1 %collective-permute-done.13 = f32[8,1,32,32]{0,3,2,1:T(8,128)S(1)} collective-permute-done((f32[8,1,32,32]{0,3,2,1:T(8,128)S(1)}, f32[8,1,32,32]{0,3,2,1:T(8,128)S(1)}, u32[]{:S(2)}, u32[]{:S(2)}) %collective-permute-start.13) | collective-permute-done | bytes 32800 | tf_op jit(solution)/shard_map/ppermute | solution.py:22
  191.8 4.4 fusion.317
  198.3 3.6 collective-permute-start.14
  202.4 9.8 %collective-permute-done.15 = f32[8,1,32,32]{0,3,2,1:T(8,128)S(1)} collective-permute-done((f32[8,1,32,32]{0,3,2,1:T(8,128)S(1)}, f32[8,1,32,32]{0,3,2,1:T(8,128)S(1)}, u32[]{:S(2)}, u32[]{:S(2)}) %collective-permute-start.15) | collective-permute-done | bytes 32800 | tf_op jit(solution)/shard_map/ppermute | solution.py:22
  212.2 5.5 %fusion.316 = f32[8,4,32,32]{0,3,2,1:T(8,128)} fusion(f32[8,4,32,32]{0,3,2,1:T(8,128)S(1)} %fusion.317, f32[8,4,32,32]{0,3,2,1:T(8,128)S(1)} %copy-done.7, f32[8,3,32,32]{0,3,2,1:T(8,128)S(1)} %get-tuple-element.63, f32[8,3,32,32]{0,3,2,1:T(8,128)S(1)} %get-tuple-element.62, f32[8,1,32,32]{0,3,2,1:T(8,128)S(1)} %collective-permute-done.14, ...), kind=kLoop, calls=%fused_computation.411 | loop fusion | flops 786432 | bytes 770056 | tf_op jit(solution)/shard_map/jit(_where)/select_n | solution.py:151
  217.7 3.0 copy.145
  223.2 3.0 copy.146
  230.2 3.8 collective-permute-start.16
  234.2 8.5 %collective-permute-done.17 = f32[8,1,128,128]{2,0,3,1:T(8,128)S(1)} collective-permute-done((f32[8,1,128,128]{2,0,3,1:T(8,128)S(1)}, f32[8,1,128,128]{2,0,3,1:T(8,128)S(1)}, u32[]{:S(2)}, u32[]{:S(2)}) %collective-permute-start.17) | collective-permute-done | bytes 524320 | tf_op jit(solution)/shard_map/ppermute | solution.py:22
  242.7 2.7 fusion.324
  247.4 3.9 collective-permute-start.18
  251.5 8.8 %collective-permute-done.19 = f32[8,1,128,128]{2,0,3,1:T(8,128)S(1)} collective-permute-done((f32[8,1,128,128]{2,0,3,1:T(8,128)S(1)}, f32[8,1,128,128]{2,0,3,1:T(8,128)S(1)}, u32[]{:S(2)}, u32[]{:S(2)}) %collective-permute-start.19) | collective-permute-done | bytes 524320 | tf_op jit(solution)/shard_map/ppermute | solution.py:22
  265.0 3.6 collective-permute-start.20
  268.8 8.5 %collective-permute-done.21 = f32[8,1,128,128]{2,0,3,1:T(8,128)S(1)} collective-permute-done((f32[8,1,128,128]{2,0,3,1:T(8,128)S(1)}, f32[8,1,128,128]{2,0,3,1:T(8,128)S(1)}, u32[]{:S(2)}, u32[]{:S(2)}) %collective-permute-start.21) | collective-permute-done | bytes 524320 | tf_op jit(solution)/shard_map/ppermute | solution.py:22
  277.4 2.7 fusion.322
  282.0 3.6 collective-permute-start.22
  285.9 8.4 %collective-permute-done.23 = f32[8,1,128,128]{2,0,3,1:T(8,128)S(1)} collective-permute-done((f32[8,1,128,128]{2,0,3,1:T(8,128)S(1)}, f32[8,1,128,128]{2,0,3,1:T(8,128)S(1)}, u32[]{:S(2)}, u32[]{:S(2)}) %collective-permute-start.23) | collective-permute-done | bytes 524320 | tf_op jit(solution)/shard_map/ppermute | solution.py:22
  299.0 3.6 collective-permute-start.24
  302.8 8.5 %collective-permute-done.25 = f32[8,1,128,128]{2,0,3,1:T(8,128)S(1)} collective-permute-done((f32[8,1,128,128]{2,0,3,1:T(8,128)S(1)}, f32[8,1,128,128]{2,0,3,1:T(8,128)S(1)}, u32[]{:S(2)}, u32[]{:S(2)}) %collective-permute-start.25) | collective-permute-done | bytes 524320 | tf_op jit(solution)/shard_map/ppermute | solution.py:22
  311.4 3.6 fusion.209
  315.0 26.3 %copy.147 = f32[8,4,128,128]{0,3,2,1:T(8,128)} copy(f32[8,4,128,128]{2,0,3,1:T(8,128)} %fusion.209) | data formatting | bytes 4194304 | tf_op jit(solution)/shard_map/jit(_where)/select_n | solution.py:140
  341.3 14.4 %reduce_sum.58 = f32[8,4,32,32]{0,3,2,1:T(8,128)} reduce(f32[8,4,32,4,32,4]{0,5,4,3,2,1:T(4,128)} %bitcast.89, f32[]{:T(128)} %constant.82.clone.1), dimensions={3,5}, to_apply=%region_4.5 | reduce | flops 491520 | bytes 2228228 | tf_op jit(solution)/shard_map/reduce_sum | solution.py:73
  355.7 9.8 %divide_select_fusion = f32[8,4,32,32]{0,3,2,1:T(8,128)S(1)} fusion(f32[8,4,32,32]{0,3,2,1:T(8,128)} %reduce_sum.58, f32[4,32,32]{2,1,0:T(8,128)S(1)} %get-tuple-element.98, pred[4]{0:T(512)(128)(4,1)S(1)} %iota_compare_fusion.1, f32[8,4,32,32]{0,3,2,1:T(8,128)} %copy-done.22, f32[4,32,32]{2,1,0:T(8,128)} %get-tuple-element.102, ...), kind=kLoop, calls=%fused_computation.405 | loop fusion | flops 720896 | bytes 573448 | tf_op jit(solution)/shard_map/jit(_where)/select_n | solution.py:151
  367.5 3.8 collective-permute-start.26
  371.8 8.1 %collective-permute-done.27 = f32[8,1,32,32]{0,3,2,1:T(8,128)S(1)} collective-permute-done((f32[8,1,32,32]{0,3,2,1:T(8,128)S(1)}, f32[8,1,32,32]{0,3,2,1:T(8,128)S(1)}, u32[]{:S(2)}, u32[]{:S(2)}) %collective-permute-start.27) | collective-permute-done | bytes 32800 | tf_op jit(solution)/shard_map/ppermute | solution.py:22
  380.0 4.5 fusion.315
  386.4 3.6 collective-permute-start.28
  390.6 8.2 %collective-permute-done.29 = f32[8,1,32,32]{0,3,2,1:T(8,128)S(1)} collective-permute-done((f32[8,1,32,32]{0,3,2,1:T(8,128)S(1)}, f32[8,1,32,32]{0,3,2,1:T(8,128)S(1)}, u32[]{:S(2)}, u32[]{:S(2)}) %collective-permute-start.29) | collective-permute-done | bytes 32800 | tf_op jit(solution)/shard_map/ppermute | solution.py:22
  398.8 4.4 fusion.314
  405.3 3.9 collective-permute-start.30
  409.6 7.9 %collective-permute-done.31 = f32[8,1,32,32]{0,3,2,1:T(8,128)S(1)} collective-permute-done((f32[8,1,32,32]{0,3,2,1:T(8,128)S(1)}, f32[8,1,32,32]{0,3,2,1:T(8,128)S(1)}, u32[]{:S(2)}, u32[]{:S(2)}) %collective-permute-start.31) | collective-permute-done | bytes 32800 | tf_op jit(solution)/shard_map/ppermute | solution.py:22
  417.5 5.5 %fusion.313 = f32[8,4,32,32]{0,3,2,1:T(8,128)} fusion(f32[8,4,32,32]{0,3,2,1:T(8,128)S(1)} %fusion.314, f32[8,4,32,32]{0,3,2,1:T(8,128)S(1)} %copy-done.6, f32[8,3,32,32]{0,3,2,1:T(8,128)S(1)} %get-tuple-element.31, f32[8,3,32,32]{0,3,2,1:T(8,128)S(1)} %get-tuple-element.30, f32[8,1,32,32]{0,3,2,1:T(8,128)S(1)} %collective-permute-done.30, ...), kind=kLoop, calls=%fused_computation.408 | loop fusion | flops 786432 | bytes 770056 | tf_op jit(solution)/shard_map/jit(_where)/select_n | solution.py:151
  423.1 3.0 copy.148
  428.6 3.0 copy.149
  437.8 3.6 collective-permute-start.32
  441.4 2.9 copy.152
  446.6 3.9 collective-permute-done.33
  450.5 4.0 fusion.320
  456.6 3.6 collective-permute-start.34
  462.4 6.5 %collective-permute-done.35 = f32[8,1,128,128]{2,0,3,1:T(8,128)S(1)} collective-permute-done((f32[8,1,128,128]{2,0,3,1:T(8,128)S(1)}, f32[8,1,128,128]{2,0,3,1:T(8,128)S(1)}, u32[]{:S(2)}, u32[]{:S(2)}) %collective-permute-start.35) | collective-permute-done | bytes 524320 | tf_op jit(solution)/shard_map/ppermute | solution.py:22
  475.9 3.8 collective-permute-start.36
  485.2 3.6 collective-permute-done.37
  488.8 5.2 %fusion.254 = f32[4,128,128]{1,2,0:T(8,128)S(1)} fusion(f32[8,4,128,128]{2,0,3,1:T(8,128)S(1)} %copy-done.17, f32[8,4,128,128]{2,0,3,1:T(8,128)S(1)} %copy-done.1, f32[8,3,128,128]{2,0,3,1:T(8,128)S(1)} %copy-done.25, f32[8,1,128,128]{2,0,3,1:T(8,128)S(1)} %copy.163, f32[8,3,128,128]{2,0,3,1:T(8,128)S(1)} %get-tuple-element.19, ...), kind=kLoop, calls=%fused_computation.330 | loop fusion | flops 14614528 | bytes 12845060 | tf_op jit(solution)/shard_map/reduce_sum | solution.py:162
  (216 shorter events, 108.6 us)
Async XLA Ops:
  1.5 49.3 %collective-permute-start.3 = (f32[8,1,128,128]{2,0,3,1:T(8,128)}, f32[8,1,128,128]{2,0,3,1:T(8,128)}, u32[]{:S(2)}, u32[]{:S(2)}) collective-permute-start(f32[8,1,128,128]{2,0,3,1:T(8,128)} %dynamic_slice.70), channel_id=1, source_target_pairs={{1,0},{2,1},{3,2},{4,3},{5,4},{6,5},{7,6},{8,7},{9,8},{10,9},{11,1... | collective-permute-start | bytes 1572872 | tf_op jit(solution)/shard_map/ppermute | solution.py:22
  4.0 46.7 %collective-permute-start.1 = (f32[8,1,128,128]{2,0,3,1:T(8,128)}, f32[8,1,128,128]{2,0,3,1:T(8,128)}, u32[]{:S(2)}, u32[]{:S(2)}) collective-permute-start(f32[8,1,128,128]{2,0,3,1:T(8,128)} %dynamic_slice.70), channel_id=1, source_target_pairs={{0,1},{1,2},{2,3},{3,4},{4,5},{5,6},{6,7},{7,8},{8,9},{9,10},{10,1... | collective-permute-start | bytes 1572872 | tf_op jit(solution)/shard_map/ppermute | solution.py:21
  11.9 10.1 %copy-start.23 = (f32[4,128,128]{2,1,0:T(8,128)S(1)}, f32[4,128,128]{2,1,0:T(8,128)}, u32[]{:S(2)}) copy-start(f32[4,128,128]{2,1,0:T(8,128)} %param.4) | copy-start | bytes 786436
  13.1 26.5 %collective-permute-start.2 = (f32[9,1,128,128]{3,2,1,0:T(8,128)}, f32[9,1,128,128]{3,2,1,0:T(8,128)S(1)}, u32[]{:S(2)}, u32[]{:S(2)}) collective-permute-start(f32[9,1,128,128]{3,2,1,0:T(8,128)} %get-tuple-element.83), channel_id=1, source_target_pairs={{1,0},{2,1},{3,2},{4,3},{5,4},{6,5},{7,6},{8,7},{9,8},{10,9},{11,1... | collective-permute-start | bytes 1769480 | tf_op jit(solution)/shard_map/ppermute | solution.py:22
  15.0 28.4 %collective-permute-start = (f32[9,1,128,128]{3,2,1,0:T(8,128)}, f32[9,1,128,128]{3,2,1,0:T(8,128)S(1)}, u32[]{:S(2)}, u32[]{:S(2)}) collective-permute-start(f32[9,1,128,128]{3,2,1,0:T(8,128)} %get-tuple-element.82), channel_id=1, source_target_pairs={{0,1},{1,2},{2,3},{3,4},{4,5},{5,6},{6,7},{7,8},{8,9},{9,10},{10,1... | collective-permute-start | bytes 1769480 | tf_op jit(solution)/shard_map/ppermute | solution.py:21
  19.6 126.8 %collective-permute-start.9 = (f32[8,1,32,32]{0,3,2,1:T(8,128)}, f32[8,1,32,32]{0,3,2,1:T(8,128)}, u32[]{:S(2)}, u32[]{:S(2)}) collective-permute-start(f32[8,1,32,32]{0,3,2,1:T(8,128)} %dynamic_slice.73), channel_id=1, source_target_pairs={{1,0},{2,1},{3,2},{4,3},{5,4},{6,5},{7,6},{8,7},{9,8},{10,9},{11,1... | collective-permute-start | bytes 98312 | tf_op jit(solution)/shard_map/ppermute | solution.py:22
  39.7 106.7 %collective-permute-start.8 = (f32[8,1,32,32]{0,3,2,1:T(8,128)}, f32[8,1,32,32]{0,3,2,1:T(8,128)}, u32[]{:S(2)}, u32[]{:S(2)}) collective-permute-start(f32[8,1,32,32]{0,3,2,1:T(8,128)} %dynamic_slice.73), channel_id=1, source_target_pairs={{0,1},{1,2},{2,3},{3,4},{4,5},{5,6},{6,7},{7,8},{8,9},{9,10},{10,1... | collective-permute-start | bytes 98312 | tf_op jit(solution)/shard_map/ppermute | solution.py:21
  57.0 6.6 %copy-start.43 = (f32[1,1,128,128]{3,2,1,0:T(8,128)S(1)}, f32[1,1,128,128]{3,2,1,0:T(8,128)}, u32[]{:S(2)}) copy-start(f32[1,1,128,128]{3,2,1,0:T(8,128)} %get-tuple-element.86) | copy-start | bytes 196612
  58.1 21.3 %collective-permute-start.5 = (f32[8,1,128,128]{2,0,3,1:T(8,128)}, f32[8,1,128,128]{2,0,3,1:T(8,128)}, u32[]{:S(2)}, u32[]{:S(2)}) collective-permute-start(f32[8,1,128,128]{2,0,3,1:T(8,128)} %get-tuple-element.76), channel_id=1, source_target_pairs={{1,0},{2,1},{3,2},{4,3},{5,4},{6,5},{7,6},{8,7},{9,8},{10,9},{11,1... | collective-permute-start | bytes 1572872 | tf_op jit(solution)/shard_map/ppermute | solution.py:22
  61.5 17.9 %collective-permute-start.4 = (f32[8,1,128,128]{2,0,3,1:T(8,128)}, f32[8,1,128,128]{2,0,3,1:T(8,128)}, u32[]{:S(2)}, u32[]{:S(2)}) collective-permute-start(f32[8,1,128,128]{2,0,3,1:T(8,128)} %get-tuple-element.77), channel_id=1, source_target_pairs={{0,1},{1,2},{2,3},{3,4},{4,5},{5,6},{6,7},{7,8},{8,9},{9,10},{10,1... | collective-permute-start | bytes 1572872 | tf_op jit(solution)/shard_map/ppermute | solution.py:21
  83.7 18.3 %copy-start.2 = (f32[8,4,128,128]{2,0,3,1:T(8,128)}, f32[8,4,128,128]{2,0,3,1:T(8,128)S(1)}, u32[]{:S(2)}) copy-start(f32[8,4,128,128]{2,0,3,1:T(8,128)S(1)} %fusion.325) | copy-start | bytes 6291460
  83.7 6.7 %copy-start.37 = (f32[4,32,32]{2,1,0:T(8,128)S(1)}, f32[4,32,32]{2,1,0:T(8,128)}, u32[]{:S(2)}) copy-start(f32[4,32,32]{2,1,0:T(8,128)} %copy-done.36) | copy-start | bytes 49156
  83.7 6.7 %copy-start.44 = (f32[3,32,32]{2,1,0:T(8,128)S(1)}, f32[3,32,32]{2,1,0:T(8,128)}, u32[]{:S(2)}) copy-start(f32[3,32,32]{2,1,0:T(8,128)} %get-tuple-element.103) | copy-start | bytes 36868
  83.7 6.7 %copy-start.45 = (f32[1,32,32]{2,1,0:T(8,128)S(1)}, f32[1,32,32]{2,1,0:T(8,128)}, u32[]{:S(2)}) copy-start(f32[1,32,32]{2,1,0:T(8,128)} %get-tuple-element.106) | copy-start | bytes 12292
  83.8 11.4 %collective-permute-start.7 = (f32[8,1,128,128]{2,0,3,1:T(8,128)S(1)}, f32[8,1,128,128]{2,0,3,1:T(8,128)S(1)}, u32[]{:S(2)}, u32[]{:S(2)}) collective-permute-start(f32[8,1,128,128]{2,0,3,1:T(8,128)S(1)} %get-tuple-element.72), channel_id=1, source_target_pairs={{1,0},{2,1},{3,2},{4,3},{5,4},{6,5},{7,6},{8,7},{9,8},{10,9},{11,1... | collective-permute-start | bytes 1572872 | tf_op jit(solution)/shard_map/ppermute | solution.py:22
  88.2 13.8 %collective-permute-start.6 = (f32[8,1,128,128]{2,0,3,1:T(8,128)S(1)}, f32[8,1,128,128]{2,0,3,1:T(8,128)S(1)}, u32[]{:S(2)}, u32[]{:S(2)}) collective-permute-start(f32[8,1,128,128]{2,0,3,1:T(8,128)S(1)} %get-tuple-element.73), channel_id=1, source_target_pairs={{0,1},{1,2},{2,3},{3,4},{4,5},{5,6},{6,7},{7,8},{8,9},{9,10},{10,1... | collective-permute-start | bytes 1572872 | tf_op jit(solution)/shard_map/ppermute | solution.py:21
  147.9 6.2 %copy-start.22 = (f32[8,4,32,32]{0,3,2,1:T(8,128)}, f32[8,4,32,32]{0,3,2,1:T(8,128)S(1)}, u32[]{:S(2)}) copy-start(f32[8,4,32,32]{0,3,2,1:T(8,128)S(1)} %broadcast.194) | copy-start | bytes 393220
  154.2 16.9 %collective-permute-start.11 = (f32[8,1,32,32]{0,3,2,1:T(8,128)S(1)}, f32[8,1,32,32]{0,3,2,1:T(8,128)S(1)}, u32[]{:S(2)}, u32[]{:S(2)}) collective-permute-start(f32[8,1,32,32]{0,3,2,1:T(8,128)S(1)} %get-tuple-element.68), channel_id=1, source_target_pairs={{1,0},{2,1},{3,2},{4,3},{5,4},{6,5},{7,6},{8,7},{9,8},{10,9},{11,1... | collective-permute-start | bytes 98312 | tf_op jit(solution)/shard_map/ppermute | solution.py:22
  156.4 14.7 %copy-start.26 = (f32[4,32,32]{2,1,0:T(8,128)S(1)}, f32[4,32,32]{2,1,0:T(8,128)}, u32[]{:S(2)}) copy-start(f32[4,32,32]{2,1,0:T(8,128)} %get-tuple-element.99) | copy-start | bytes 49156
  156.4 14.7 %copy-start.28 = (f32[4,32,32]{2,1,0:T(8,128)S(1)}, f32[4,32,32]{2,1,0:T(8,128)}, u32[]{:S(2)}) copy-start(f32[4,32,32]{2,1,0:T(8,128)} %get-tuple-element.100) | copy-start | bytes 49156
  156.4 14.7 %copy-start.30 = (f32[4,32,32]{2,1,0:T(8,128)S(1)}, f32[4,32,32]{2,1,0:T(8,128)}, u32[]{:S(2)}) copy-start(f32[4,32,32]{2,1,0:T(8,128)} %get-tuple-element.101) | copy-start | bytes 49156
  156.5 14.7 %copy-start.32 = (f32[4,32,32]{2,1,0:T(8,128)S(1)}, f32[4,32,32]{2,1,0:T(8,128)}, u32[]{:S(2)}) copy-start(f32[4,32,32]{2,1,0:T(8,128)} %get-tuple-element.102) | copy-start | bytes 49156
  156.5 14.7 %copy-start.34 = (f32[4,32,32]{2,1,0:T(8,128)S(1)}, f32[4,32,32]{2,1,0:T(8,128)}, u32[]{:S(2)}) copy-start(f32[4,32,32]{2,1,0:T(8,128)} %fusion.349) | copy-start | bytes 49156
  156.5 14.6 %collective-permute-start.10 = (f32[8,1,32,32]{0,3,2,1:T(8,128)S(1)}, f32[8,1,32,32]{0,3,2,1:T(8,128)S(1)}, u32[]{:S(2)}, u32[]{:S(2)}) collective-permute-start(f32[8,1,32,32]{0,3,2,1:T(8,128)S(1)} %get-tuple-element.69), channel_id=1, source_target_pairs={{0,1},{1,2},{2,3},{3,4},{4,5},{5,6},{6,7},{7,8},{8,9},{9,10},{10,1... | collective-permute-start | bytes 98312 | tf_op jit(solution)/shard_map/ppermute | solution.py:21
  175.7 16.1 %collective-permute-start.13 = (f32[8,1,32,32]{0,3,2,1:T(8,128)S(1)}, f32[8,1,32,32]{0,3,2,1:T(8,128)S(1)}, u32[]{:S(2)}, u32[]{:S(2)}) collective-permute-start(f32[8,1,32,32]{0,3,2,1:T(8,128)S(1)} %get-tuple-element.64), channel_id=1, source_target_pairs={{1,0},{2,1},{3,2},{4,3},{5,4},{6,5},{7,6},{8,7},{9,8},{10,9},{11,1... | collective-permute-start | bytes 98312 | tf_op jit(solution)/shard_map/ppermute | solution.py:22
  177.6 14.2 %collective-permute-start.12 = (f32[8,1,32,32]{0,3,2,1:T(8,128)S(1)}, f32[8,1,32,32]{0,3,2,1:T(8,128)S(1)}, u32[]{:S(2)}, u32[]{:S(2)}) collective-permute-start(f32[8,1,32,32]{0,3,2,1:T(8,128)S(1)} %get-tuple-element.65), channel_id=1, source_target_pairs={{0,1},{1,2},{2,3},{3,4},{4,5},{5,6},{6,7},{7,8},{8,9},{9,10},{10,1... | collective-permute-start | bytes 98312 | tf_op jit(solution)/shard_map/ppermute | solution.py:21
  196.3 15.8 %collective-permute-start.15 = (f32[8,1,32,32]{0,3,2,1:T(8,128)S(1)}, f32[8,1,32,32]{0,3,2,1:T(8,128)S(1)}, u32[]{:S(2)}, u32[]{:S(2)}) collective-permute-start(f32[8,1,32,32]{0,3,2,1:T(8,128)S(1)} %get-tuple-element.60), channel_id=1, source_target_pairs={{1,0},{2,1},{3,2},{4,3},{5,4},{6,5},{7,6},{8,7},{9,8},{10,9},{11,1... | collective-permute-start | bytes 98312 | tf_op jit(solution)/shard_map/ppermute | solution.py:22
  198.3 13.9 %collective-permute-start.14 = (f32[8,1,32,32]{0,3,2,1:T(8,128)S(1)}, f32[8,1,32,32]{0,3,2,1:T(8,128)S(1)}, u32[]{:S(2)}, u32[]{:S(2)}) collective-permute-start(f32[8,1,32,32]{0,3,2,1:T(8,128)S(1)} %get-tuple-element.61), channel_id=1, source_target_pairs={{0,1},{1,2},{2,3},{3,4},{4,5},{5,6},{6,7},{7,8},{8,9},{9,10},{10,1... | collective-permute-start | bytes 98312 | tf_op jit(solution)/shard_map/ppermute | solution.py:21
  228.2 14.5 %collective-permute-start.17 = (f32[8,1,128,128]{2,0,3,1:T(8,128)S(1)}, f32[8,1,128,128]{2,0,3,1:T(8,128)S(1)}, u32[]{:S(2)}, u32[]{:S(2)}) collective-permute-start(f32[8,1,128,128]{2,0,3,1:T(8,128)S(1)} %get-tuple-element.56), channel_id=1, source_target_pairs={{1,0},{2,1},{3,2},{4,3},{5,4},{6,5},{7,6},{8,7},{9,8},{10,9},{11,1... | collective-permute-start | bytes 1572872 | tf_op jit(solution)/shard_map/ppermute | solution.py:22
  230.2 12.5 %copy-start.14 = (f32[4,128,128]{1,2,0:T(8,128)S(1)}, f32[4,128,128]{1,2,0:T(8,128)}, u32[]{:S(2)}) copy-start(f32[4,128,128]{1,2,0:T(8,128)} %copy.142) | copy-start | bytes 786436
  230.2 12.5 %copy-start.20 = (f32[4,128,128]{1,2,0:T(8,128)S(1)}, f32[4,128,128]{1,2,0:T(8,128)}, u32[]{:S(2)}) copy-start(f32[4,128,128]{1,2,0:T(8,128)} %copy.143) | copy-start | bytes 786436
  230.2 12.5 %collective-permute-start.16 = (f32[8,1,128,128]{2,0,3,1:T(8,128)S(1)}, f32[8,1,128,128]{2,0,3,1:T(8,128)S(1)}, u32[]{:S(2)}, u32[]{:S(2)}) collective-permute-start(f32[8,1,128,128]{2,0,3,1:T(8,128)S(1)} %get-tuple-element.57), channel_id=1, source_target_pairs={{0,1},{1,2},{2,3},{3,4},{4,5},{5,6},{6,7},{7,8},{8,9},{9,10},{10,1... | collective-permute-start | bytes 1572872 | tf_op jit(solution)/shard_map/ppermute | solution.py:21
  245.5 14.8 %collective-permute-start.19 = (f32[8,1,128,128]{2,0,3,1:T(8,128)S(1)}, f32[8,1,128,128]{2,0,3,1:T(8,128)S(1)}, u32[]{:S(2)}, u32[]{:S(2)}) collective-permute-start(f32[8,1,128,128]{2,0,3,1:T(8,128)S(1)} %get-tuple-element.52), channel_id=1, source_target_pairs={{1,0},{2,1},{3,2},{4,3},{5,4},{6,5},{7,6},{8,7},{9,8},{10,9},{11,1... | collective-permute-start | bytes 1572872 | tf_op jit(solution)/shard_map/ppermute | solution.py:22
  247.4 12.9 %collective-permute-start.18 = (f32[8,1,128,128]{2,0,3,1:T(8,128)S(1)}, f32[8,1,128,128]{2,0,3,1:T(8,128)S(1)}, u32[]{:S(2)}, u32[]{:S(2)}) collective-permute-start(f32[8,1,128,128]{2,0,3,1:T(8,128)S(1)} %get-tuple-element.53), channel_id=1, source_target_pairs={{0,1},{1,2},{2,3},{3,4},{4,5},{5,6},{6,7},{7,8},{8,9},{9,10},{10,1... | collective-permute-start | bytes 1572872 | tf_op jit(solution)/shard_map/ppermute | solution.py:21
  263.0 14.3 %collective-permute-start.21 = (f32[8,1,128,128]{2,0,3,1:T(8,128)S(1)}, f32[8,1,128,128]{2,0,3,1:T(8,128)S(1)}, u32[]{:S(2)}, u32[]{:S(2)}) collective-permute-start(f32[8,1,128,128]{2,0,3,1:T(8,128)S(1)} %get-tuple-element.48), channel_id=1, source_target_pairs={{1,0},{2,1},{3,2},{4,3},{5,4},{6,5},{7,6},{8,7},{9,8},{10,9},{11,1... | collective-permute-start | bytes 1572872 | tf_op jit(solution)/shard_map/ppermute | solution.py:22
  265.0 12.4 %collective-permute-start.20 = (f32[8,1,128,128]{2,0,3,1:T(8,128)S(1)}, f32[8,1,128,128]{2,0,3,1:T(8,128)S(1)}, u32[]{:S(2)}, u32[]{:S(2)}) collective-permute-start(f32[8,1,128,128]{2,0,3,1:T(8,128)S(1)} %get-tuple-element.49), channel_id=1, source_target_pairs={{0,1},{1,2},{2,3},{3,4},{4,5},{5,6},{6,7},{7,8},{8,9},{9,10},{10,1... | collective-permute-start | bytes 1572872 | tf_op jit(solution)/shard_map/ppermute | solution.py:21
  280.1 14.2 %collective-permute-start.23 = (f32[8,1,128,128]{2,0,3,1:T(8,128)S(1)}, f32[8,1,128,128]{2,0,3,1:T(8,128)S(1)}, u32[]{:S(2)}, u32[]{:S(2)}) collective-permute-start(f32[8,1,128,128]{2,0,3,1:T(8,128)S(1)} %get-tuple-element.44), channel_id=1, source_target_pairs={{1,0},{2,1},{3,2},{4,3},{5,4},{6,5},{7,6},{8,7},{9,8},{10,9},{11,1... | collective-permute-start | bytes 1572872 | tf_op jit(solution)/shard_map/ppermute | solution.py:22
  282.0 12.2 %collective-permute-start.22 = (f32[8,1,128,128]{2,0,3,1:T(8,128)S(1)}, f32[8,1,128,128]{2,0,3,1:T(8,128)S(1)}, u32[]{:S(2)}, u32[]{:S(2)}) collective-permute-start(f32[8,1,128,128]{2,0,3,1:T(8,128)S(1)} %get-tuple-element.45), channel_id=1, source_target_pairs={{0,1},{1,2},{2,3},{3,4},{4,5},{5,6},{6,7},{7,8},{8,9},{9,10},{10,1... | collective-permute-start | bytes 1572872 | tf_op jit(solution)/shard_map/ppermute | solution.py:21
  296.9 14.4 %copy-start.4 = (f32[8,4,128,128]{2,0,3,1:T(8,128)}, f32[8,4,128,128]{2,0,3,1:T(8,128)S(1)}, u32[]{:S(2)}) copy-start(f32[8,4,128,128]{2,0,3,1:T(8,128)S(1)} %fusion.321) | copy-start | bytes 6291460
  297.0 14.3 %collective-permute-start.25 = (f32[8,1,128,128]{2,0,3,1:T(8,128)S(1)}, f32[8,1,128,128]{2,0,3,1:T(8,128)S(1)}, u32[]{:S(2)}, u32[]{:S(2)}) collective-permute-start(f32[8,1,128,128]{2,0,3,1:T(8,128)S(1)} %get-tuple-element.40), channel_id=1, source_target_pairs={{1,0},{2,1},{3,2},{4,3},{5,4},{6,5},{7,6},{8,7},{9,8},{10,9},{11,1... | collective-permute-start | bytes 1572872 | tf_op jit(solution)/shard_map/ppermute | solution.py:22
  299.0 12.4 %collective-permute-start.24 = (f32[8,1,128,128]{2,0,3,1:T(8,128)S(1)}, f32[8,1,128,128]{2,0,3,1:T(8,128)S(1)}, u32[]{:S(2)}, u32[]{:S(2)}) collective-permute-start(f32[8,1,128,128]{2,0,3,1:T(8,128)S(1)} %get-tuple-element.41), channel_id=1, source_target_pairs={{0,1},{1,2},{2,3},{3,4},{4,5},{5,6},{6,7},{7,8},{8,9},{9,10},{10,1... | collective-permute-start | bytes 1572872 | tf_op jit(solution)/shard_map/ppermute | solution.py:21
  365.5 14.4 %collective-permute-start.27 = (f32[8,1,32,32]{0,3,2,1:T(8,128)S(1)}, f32[8,1,32,32]{0,3,2,1:T(8,128)S(1)}, u32[]{:S(2)}, u32[]{:S(2)}) collective-permute-start(f32[8,1,32,32]{0,3,2,1:T(8,128)S(1)} %get-tuple-element.36), channel_id=1, source_target_pairs={{1,0},{2,1},{3,2},{4,3},{5,4},{6,5},{7,6},{8,7},{9,8},{10,9},{11,1... | collective-permute-start | bytes 98312 | tf_op jit(solution)/shard_map/ppermute | solution.py:22
  367.5 12.4 %copy-start.6 = (f32[8,4,32,32]{0,3,2,1:T(8,128)S(1)}, f32[8,4,32,32]{0,3,2,1:T(8,128)}, u32[]{:S(2)}) copy-start(f32[8,4,32,32]{0,3,2,1:T(8,128)} %reduce_sum.58) | copy-start | bytes 393220
  367.5 12.4 %copy-start.27 = (f32[4,32,32]{2,1,0:T(8,128)S(1)}, f32[4,32,32]{2,1,0:T(8,128)}, u32[]{:S(2)}) copy-start(f32[4,32,32]{2,1,0:T(8,128)} %get-tuple-element.99) | copy-start | bytes 49156
  367.5 12.4 %copy-start.29 = (f32[4,32,32]{2,1,0:T(8,128)S(1)}, f32[4,32,32]{2,1,0:T(8,128)}, u32[]{:S(2)}) copy-start(f32[4,32,32]{2,1,0:T(8,128)} %get-tuple-element.100) | copy-start | bytes 49156
  367.5 12.4 %copy-start.31 = (f32[4,32,32]{2,1,0:T(8,128)S(1)}, f32[4,32,32]{2,1,0:T(8,128)}, u32[]{:S(2)}) copy-start(f32[4,32,32]{2,1,0:T(8,128)} %get-tuple-element.101) | copy-start | bytes 49156
  367.5 12.4 %copy-start.33 = (f32[4,32,32]{2,1,0:T(8,128)S(1)}, f32[4,32,32]{2,1,0:T(8,128)}, u32[]{:S(2)}) copy-start(f32[4,32,32]{2,1,0:T(8,128)} %get-tuple-element.102) | copy-start | bytes 49156
  367.5 12.4 %copy-start.35 = (f32[4,32,32]{2,1,0:T(8,128)S(1)}, f32[4,32,32]{2,1,0:T(8,128)}, u32[]{:S(2)}) copy-start(f32[4,32,32]{2,1,0:T(8,128)} %fusion.349) | copy-start | bytes 49156
  367.5 12.4 %collective-permute-start.26 = (f32[8,1,32,32]{0,3,2,1:T(8,128)S(1)}, f32[8,1,32,32]{0,3,2,1:T(8,128)S(1)}, u32[]{:S(2)}, u32[]{:S(2)}) collective-permute-start(f32[8,1,32,32]{0,3,2,1:T(8,128)S(1)} %get-tuple-element.37), channel_id=1, source_target_pairs={{0,1},{1,2},{2,3},{3,4},{4,5},{5,6},{6,7},{7,8},{8,9},{9,10},{10,1... | collective-permute-start | bytes 98312 | tf_op jit(solution)/shard_map/ppermute | solution.py:21
  384.5 14.3 %collective-permute-start.29 = (f32[8,1,32,32]{0,3,2,1:T(8,128)S(1)}, f32[8,1,32,32]{0,3,2,1:T(8,128)S(1)}, u32[]{:S(2)}, u32[]{:S(2)}) collective-permute-start(f32[8,1,32,32]{0,3,2,1:T(8,128)S(1)} %get-tuple-element.32), channel_id=1, source_target_pairs={{1,0},{2,1},{3,2},{4,3},{5,4},{6,5},{7,6},{8,7},{9,8},{10,9},{11,1... | collective-permute-start | bytes 98312 | tf_op jit(solution)/shard_map/ppermute | solution.py:22
  386.4 12.4 %collective-permute-start.28 = (f32[8,1,32,32]{0,3,2,1:T(8,128)S(1)}, f32[8,1,32,32]{0,3,2,1:T(8,128)S(1)}, u32[]{:S(2)}, u32[]{:S(2)}) collective-permute-start(f32[8,1,32,32]{0,3,2,1:T(8,128)S(1)} %get-tuple-element.33), channel_id=1, source_target_pairs={{0,1},{1,2},{2,3},{3,4},{4,5},{5,6},{6,7},{7,8},{8,9},{9,10},{10,1... | collective-permute-start | bytes 98312 | tf_op jit(solution)/shard_map/ppermute | solution.py:21
  403.3 14.2 %collective-permute-start.31 = (f32[8,1,32,32]{0,3,2,1:T(8,128)S(1)}, f32[8,1,32,32]{0,3,2,1:T(8,128)S(1)}, u32[]{:S(2)}, u32[]{:S(2)}) collective-permute-start(f32[8,1,32,32]{0,3,2,1:T(8,128)S(1)} %get-tuple-element.28), channel_id=1, source_target_pairs={{1,0},{2,1},{3,2},{4,3},{5,4},{6,5},{7,6},{8,7},{9,8},{10,9},{11,1... | collective-permute-start | bytes 98312 | tf_op jit(solution)/shard_map/ppermute | solution.py:22
  405.3 12.3 %collective-permute-start.30 = (f32[8,1,32,32]{0,3,2,1:T(8,128)S(1)}, f32[8,1,32,32]{0,3,2,1:T(8,128)S(1)}, u32[]{:S(2)}, u32[]{:S(2)}) collective-permute-start(f32[8,1,32,32]{0,3,2,1:T(8,128)S(1)} %get-tuple-element.29), channel_id=1, source_target_pairs={{0,1},{1,2},{2,3},{3,4},{4,5},{5,6},{6,7},{7,8},{8,9},{9,10},{10,1... | collective-permute-start | bytes 98312 | tf_op jit(solution)/shard_map/ppermute | solution.py:21
  435.9 14.6 %collective-permute-start.33 = (f32[8,1,128,128]{2,0,3,1:T(8,128)}, f32[8,1,128,128]{2,0,3,1:T(8,128)}, u32[]{:S(2)}, u32[]{:S(2)}) collective-permute-start(f32[8,1,128,128]{2,0,3,1:T(8,128)} %get-tuple-element.24), channel_id=1, source_target_pairs={{1,0},{2,1},{3,2},{4,3},{5,4},{6,5},{7,6},{8,7},{9,8},{10,9},{11,1... | collective-permute-start | bytes 1572872 | tf_op jit(solution)/shard_map/ppermute | solution.py:22
  437.8 12.7 %collective-permute-start.32 = (f32[8,1,128,128]{2,0,3,1:T(8,128)}, f32[8,1,128,128]{2,0,3,1:T(8,128)}, u32[]{:S(2)}, u32[]{:S(2)}) collective-permute-start(f32[8,1,128,128]{2,0,3,1:T(8,128)} %get-tuple-element.25), channel_id=1, source_target_pairs={{0,1},{1,2},{2,3},{3,4},{4,5},{5,6},{6,7},{7,8},{8,9},{9,10},{10,1... | collective-permute-start | bytes 1572872 | tf_op jit(solution)/shard_map/ppermute | solution.py:21
  444.3 6.1 %copy-start.11 = (f32[8,4,128,128]{2,0,3,1:T(8,128)S(1)}, f32[8,4,128,128]{2,0,3,1:T(8,128)}, u32[]{:S(2)}) copy-start(f32[8,4,128,128]{2,0,3,1:T(8,128)} %copy-done.10) | copy-start | bytes 6291460
  444.3 6.1 %copy-start.15 = (f32[4,128,128]{1,2,0:T(8,128)S(1)}, f32[4,128,128]{1,2,0:T(8,128)}, u32[]{:S(2)}) copy-start(f32[4,128,128]{1,2,0:T(8,128)} %copy.142) | copy-start | bytes 786436
  444.3 6.1 %copy-start.21 = (f32[4,128,128]{1,2,0:T(8,128)S(1)}, f32[4,128,128]{1,2,0:T(8,128)}, u32[]{:S(2)}) copy-start(f32[4,128,128]{1,2,0:T(8,128)} %copy.143) | copy-start | bytes 786436
  454.5 14.3 %collective-permute-start.35 = (f32[8,1,128,128]{2,0,3,1:T(8,128)S(1)}, f32[8,1,128,128]{2,0,3,1:T(8,128)S(1)}, u32[]{:S(2)}, u32[]{:S(2)}) collective-permute-start(f32[8,1,128,128]{2,0,3,1:T(8,128)S(1)} %get-tuple-element.20), channel_id=1, source_target_pairs={{1,0},{2,1},{3,2},{4,3},{5,4},{6,5},{7,6},{8,7},{9,8},{10,9},{11,1... | collective-permute-start | bytes 1572872 | tf_op jit(solution)/shard_map/ppermute | solution.py:22
  456.6 12.3 %collective-permute-start.34 = (f32[8,1,128,128]{2,0,3,1:T(8,128)S(1)}, f32[8,1,128,128]{2,0,3,1:T(8,128)S(1)}, u32[]{:S(2)}, u32[]{:S(2)}) collective-permute-start(f32[8,1,128,128]{2,0,3,1:T(8,128)S(1)} %get-tuple-element.21), channel_id=1, source_target_pairs={{0,1},{1,2},{2,3},{3,4},{4,5},{5,6},{6,7},{7,8},{8,9},{9,10},{10,1... | collective-permute-start | bytes 1572872 | tf_op jit(solution)/shard_map/ppermute | solution.py:21
  472.9 6.8 %copy-start.40 = (f32[9,1,128,128]{3,2,1,0:T(8,128)S(1)}, f32[9,1,128,128]{3,2,1,0:T(8,128)}, u32[]{:S(2)}) copy-start(f32[9,1,128,128]{3,2,1,0:T(8,128)} %copy-done.39) | copy-start | bytes 1769476
  474.0 14.8 %collective-permute-start.37 = (f32[8,1,128,128]{2,0,3,1:T(8,128)}, f32[8,1,128,128]{2,0,3,1:T(8,128)}, u32[]{:S(2)}, u32[]{:S(2)}) collective-permute-start(f32[8,1,128,128]{2,0,3,1:T(8,128)} %get-tuple-element.14), channel_id=1, source_target_pairs={{1,0},{2,1},{3,2},{4,3},{5,4},{6,5},{7,6},{8,7},{9,8},{10,9},{11,1... | collective-permute-start | bytes 1572872 | tf_op jit(solution)/shard_map/ppermute | solution.py:22
  475.9 7.3 %copy-start.1 = (f32[8,4,128,128]{2,0,3,1:T(8,128)S(1)}, f32[8,4,128,128]{2,0,3,1:T(8,128)}, u32[]{:S(2)}) copy-start(f32[8,4,128,128]{2,0,3,1:T(8,128)} %copy-done) | copy-start | bytes 6291460
  475.9 12.9 %collective-permute-start.36 = (f32[8,1,128,128]{2,0,3,1:T(8,128)}, f32[8,1,128,128]{2,0,3,1:T(8,128)}, u32[]{:S(2)}, u32[]{:S(2)}) collective-permute-start(f32[8,1,128,128]{2,0,3,1:T(8,128)} %get-tuple-element.15), channel_id=1, source_target_pairs={{0,1},{1,2},{2,3},{3,4},{4,5},{5,6},{6,7},{7,8},{8,9},{9,10},{10,1... | collective-permute-start | bytes 1572872 | tf_op jit(solution)/shard_map/ppermute | solution.py:21
  (20 other events, 48.5 us)
where the time goes:
time: 505 us; the launch traced here: 495 us
  local copies, waits for them, and re-layouts  137 us (27%)
  other arithmetic  125 us (25%)
  waiting for transfers between devices  121 us (24%)
  starting transfers between devices  109 us (22%)
    ppermute x19, waiting for transfers between devices, extended_2(): after = lax.ppermute(leading, axis, down)  115 us
    ppermute x19, starting transfers between devices, extended_2(): before = lax.ppermute(last, axis, up)  66.6 us
    select_n x2, local copies, waits for them, and re-layouts, shards(): residue = jnp.where(alive_mask, residue, 0.0)  52.5 us
    select_n x8, other arithmetic, shards(): correction = jnp.where(alive_mask, coarse_updated, 0.0)  44.8 us
    ppermute x19, starting transfers between devices, extended_2(): after = lax.ppermute(leading, axis, down)  42 us
    reduce_sum x2, other arithmetic, block_sum(): values.reshape(shape[0], shape[1], shape[2] // 4, 4, shape[3] // 4, 4)  28.8 us
    select_n x8, other arithmetic, smooth(): return jnp.where(alive_mask, updated, 0.0)  25.2 us
    another operation x3, local copies, waits for them, and re-layouts, block_mean(): values.reshape(shape[0], shape[1], shape[2] // 4, 4, shape[3] // 4, 4)  17 us
  transfers between devices with their start and end apart: 38, of which 16 were waited for; matrix products, arithmetic and copies ran while one was open for 24% of the time, Pallas kernels for 0%

commit v1 on v0

v1 whole, which is shorter than its diff:
```python
import functools

import jax
import jax.numpy as jnp
from jax import lax
from jax.experimental import pallas as pl
from jax.experimental.pallas import tpu as pltpu
from jax.sharding import PartitionSpec as P

OMEGA = 0.8
F32 = jnp.float32
PAD = 8
RB = 32
CH = 2
STEPS = 8
CSTEPS = 8


def dot(a, b):
    return jnp.dot(a, b, precision=lax.Precision.HIGHEST, preferred_element_type=F32)


def kernel(n_ref, cond, fwd, rhs, adj, grad,
           w, dg, bs, va, vb, hlo, hhi, sup, sdn, fhlo, fhhi, fsup, fsdn,
           qm, qt, cw, cwb, cres, cbs, ce, chlo, chhi, csup, csdn,
           kup, kdn, klo, khi, plo, phi, rlo, rhi, sy, sz, sfa, sx, rbuf,
           up_send, up_recv, dn_send, dn_recv, cup_send, cup_recv, cdn_send, cdn_recv,
           mup_send, mup_recv, mdn_send, mdn_recv):
    slots, ny, nz = cond.shape
    nsrc = fwd.shape[0]
    half = nsrc // 2
    chunks = nsrc // CH
    cy = ny // 4
    pos = lax.axis_index("space")
    peers = lax.axis_size("space")
    n = n_ref[0]
    top = jnp.maximum(n - 1, 0)
    has_lo = pos > 0
    has_hi = pos < peers - 1

    def up_copy(src, dst, ss, rs):
        return pltpu.make_async_remote_copy(
            src_ref=src, dst_ref=dst, send_sem=ss, recv_sem=rs,
            device_id={"space": pos + 1}, device_id_type=pl.DeviceIdType.MESH)

    def dn_copy(src, dst, ss, rs):
        return pltpu.make_async_remote_copy(
            src_ref=src, dst_ref=dst, send_sem=ss, recv_sem=rs,
            device_id={"space": pos - 1}, device_id_type=pl.DeviceIdType.MESH)

    barrier = pltpu.get_barrier_semaphore()

    @pl.when(has_lo)
    def _():
        pl.semaphore_signal(barrier, inc=1, device_id={"space": pos - 1},
                            device_id_type=pl.DeviceIdType.MESH)

    @pl.when(has_hi)
    def _():
        pl.semaphore_signal(barrier, inc=1, device_id={"space": pos + 1},
                            device_id_type=pl.DeviceIdType.MESH)

    pl.semaphore_wait(barrier, jnp.where(has_lo, 1, 0) + jnp.where(has_hi, 1, 0))

    def fine(step, c):
        part = pl.ds(c * CH, CH)
        return (lambda: up_copy(sup.at[step, part], hlo.at[step, part],
                                up_send.at[step, c], up_recv.at[step, c]),
                lambda: dn_copy(sdn.at[step, part], hhi.at[step, part],
                                dn_send.at[step, c], dn_recv.at[step, c]))

    def coarse(k):
        return (lambda: up_copy(csup.at[k], chlo.at[k], cup_send.at[k], cup_recv.at[k]),
                lambda: dn_copy(csdn.at[k], chhi.at[k], cdn_send.at[k], cdn_recv.at[k]))

    def misc(i, us, ud, ds, dd):
        return (lambda: up_copy(us, ud, mup_send.at[i], mup_recv.at[i]),
                lambda: dn_copy(ds, dd, mdn_send.at[i], mdn_recv.at[i]))

    cond_pair = misc(0, kup, klo, kdn, khi)
    fwd_pair = misc(1, fsup, fhlo, fsdn, fhhi)
    prod_pair = misc(2, phi, rlo, plo, rhi)

    def start(pair, up=True, dn=True):
        if up:
            @pl.when(has_hi)
            def _():
                pair[0]().start()
        if dn:
            @pl.when(has_lo)
            def _():
                pair[1]().start()

    def wait_recv(pair, up=True, dn=True):
        if up:
            @pl.when(has_lo)
            def _():
                pair[0]().wait_recv()
        if dn:
            @pl.when(has_hi)
            def _():
                pair[1]().wait_recv()

    def wait_send(pair, up=True, dn=True):
        if up:
            @pl.when(has_hi)
            def _():
                pair[0]().wait_send()
        if dn:
            @pl.when(has_lo)
            def _():
                pair[1]().wait_send()

    kup[...] = cond[top]
    kdn[...] = cond[0]
    start(cond_pair)

    plane = jnp.zeros((ny, nz), F32)

    @pl.when(jnp.logical_not(has_lo))
    def _():
        klo[...] = plane
        chlo[...] = jnp.zeros_like(chlo)
        fhlo[...] = jnp.zeros_like(fhlo)

        @pl.loop(0, STEPS)
        def _(k):
            hlo[k] = jnp.zeros(hlo.shape[1:], F32)

    @pl.when(jnp.logical_not(has_hi))
    def _():
        khi[...] = plane
        chhi[...] = jnp.zeros_like(chhi)
        fhhi[...] = jnp.zeros_like(fhhi)

        @pl.loop(0, STEPS)
        def _(k):
            hhi[k] = jnp.zeros(hhi.shape[1:], F32)

    edge = jnp.zeros((slots, PAD, nz), F32)

    @pl.loop(0, nsrc)
    def _(s):
        for buf in (bs, va, vb):
            buf[s, :, :PAD] = edge
            buf[s, :, PAD + ny:] = edge

    row = lax.broadcasted_iota(jnp.int32, (ny, nz), 0)
    lane = lax.broadcasted_iota(jnp.int32, (ny, nz), 1)
    for s4 in range(4):
        qm[s4] = jnp.where(row // 4 + 32 * s4 == lane, 1.0, 0.0).astype(F32)
        qt[s4] = jnp.where(lane // 4 + 32 * s4 == row, 1.0, 0.0).astype(F32)

    @pl.loop(0, half)
    def _(s):
        fsup[s] = fwd[s, top]
        fsdn[s] = fwd[half + s, 0]

    wait_recv(cond_pair)

    for j in range(slots):
        c = cond[j]
        lo = klo[...] if j == 0 else cond[j - 1]
        above = plane if j == slots - 1 else cond[j + 1]
        hi = jnp.where(n - 1 == j, khi[...], above)
        faces = [(c + lo) * 0.5, (c + hi) * 0.5,
                 (c + jnp.where(row == 0, 0.0, pltpu.roll(c, 1, 0))) * 0.5,
                 (c + jnp.where(row == ny - 1, 0.0, pltpu.roll(c, ny - 1, 0))) * 0.5,
                 (c + jnp.where(lane == 0, 0.0, pltpu.roll(c, 1, 1))) * 0.5,
                 (c + jnp.where(lane == nz - 1, 0.0, pltpu.roll(c, nz - 1, 1))) * 0.5]
        diag = faces[0] + faces[1] + faces[2] + faces[3] + faces[4] + faces[5]
        alive = jnp.where(j < n, 1.0, 0.0)
        scale = alive * (OMEGA / diag)
        dg[j] = alive * diag * (1.0 / OMEGA)
        for i in range(4):
            w[i, j] = scale * faces[i]
        w[4, j] = jnp.where(lane == 0, 0.0, scale * faces[4])
        w[5, j] = jnp.where(lane == nz - 1, 0.0, scale * faces[5])
        w[6, j] = scale

    def stage(step, s, buf, off):
        sup[step, s] = buf[s, top, off:off + ny]
        sdn[step, s] = buf[s, 0, off:off + ny]

    @pl.loop(0, chunks)
    def _(c):
        for i in range(CH):
            s = c * CH + i
            for j in range(slots):
                bs[s, j, PAD:PAD + ny] = w[6, j] * rhs[s, j]
            stage(0, s, bs, PAD)
        start(fine(0, c))

    qall = jnp.where(row // 4 == lane % 32, 1.0 / 16.0, 0.0).astype(F32)

    def rows4(read):
        return read(0) + read(1) + read(2) + read(3)

    def every4(k):
        return pl.ds(k, cy, stride=4)

    cplanes = [rows4(lambda k, j=j: cond[j, every4(k), :]) for j in range(slots)]
    cplanes += [rows4(lambda k: klo[every4(k), :]), rows4(lambda k: khi[every4(k), :])]
    cmean = dot(jnp.concatenate(cplanes, axis=0), qall)
    cc = [cmean[j * cy:(j + 1) * cy] for j in range(slots + 2)]
    crow = lax.broadcasted_iota(jnp.int32, (cy, nz), 0)
    clane = lax.broadcasted_iota(jnp.int32, (cy, nz), 1) % 32
    for j in range(slots):
        c = cc[j]
        lo = cc[slots] if j == 0 else cc[j - 1]
        hi = jnp.where(n - 1 == j, cc[slots + 1], jnp.zeros_like(c) if j == slots - 1 else cc[j + 1])
        faces = [(c + lo) * 8.0, (c + hi) * 8.0,
                 (c + jnp.where(crow == 0, 0.0, pltpu.roll(c, 1, 0))) * 0.5,
                 (c + jnp.where(crow == cy - 1, 0.0, pltpu.roll(c, cy - 1, 0))) * 0.5,
                 (c + jnp.where(clane == 0, 0.0, pltpu.roll(c, 1, 1))) * 0.5,
                 (c + jnp.where(clane == 31, 0.0, pltpu.roll(c, nz - 1, 1))) * 0.5]
        diag = faces[0] + faces[1] + faces[2] + faces[3] + faces[4] + faces[5]
        scale = jnp.where(j < n, 1.0, 0.0) * (OMEGA / diag)
        cw[0, j] = scale * faces[0]
        cw[1, j] = scale * faces[1]
        cw[2, j] = jnp.where(crow == 0, 0.0, scale * faces[2])
        cw[3, j] = jnp.where(crow == cy - 1, 0.0, scale * faces[3])
        cw[4, j] = jnp.where(clane == 0, 0.0, scale * faces[4])
        cw[5, j] = jnp.where(clane == 31, 0.0, scale * faces[5])
        cwb[pl.ds(j * cy, cy), :] = scale

    def change(src, step, s, j, r0, wts, keep):
        o = PAD + r0
        rows = slice(o, o + RB)
        v = src[s, j, rows]
        lo = hlo[step, s, r0:r0 + RB] if j == 0 else src[s, j - 1, rows]
        edge_hi = hhi[step, s, r0:r0 + RB]
        above = jnp.zeros_like(edge_hi) if j == slots - 1 else src[s, j + 1, rows]
        hi = jnp.where(n - 1 == j, edge_hi, above)
        acc = bs[s, j, rows] + keep * v
        acc = acc + wts[0] * lo + wts[1] * hi
        acc = acc + wts[2] * src[s, j, o - 1:o - 1 + RB] + wts[3] * src[s, j, o + 1:o + 1 + RB]
        return acc + wts[4] * pltpu.roll(v, 1, 1) + wts[5] * pltpu.roll(v, nz - 1, 1)

    def weights(j, r0):
        return [w[i, j, r0:r0 + RB] for i in range(6)]

    def sweep(src, dst, off, step, prepare=None):
        @pl.loop(0, chunks)
        def _(c):
            if prepare is None:
                wait_recv(fine(step, c))
            else:
                prepare(c)
            for j in range(slots):
                for r0 in range(0, ny, RB):
                    wts = weights(j, r0)
                    for i in range(CH):
                        s = c * CH + i
                        dst[s, j, off + r0:off + r0 + RB] = change(
                            src, step, s, j, r0, wts, 1.0 - OMEGA)
            for i in range(CH):
                stage(step + 1, c * CH + i, dst, off)
            if step + 1 < STEPS - 1:
                start(fine(step + 1, c))
            else:
                first = c < chunks // 2

                @pl.when(first)
                def _():
                    start(fine(step + 1, c), dn=False)

                @pl.when(jnp.logical_not(first))
                def _():
                    start(fine(step + 1, c), up=False)

    def coarse_solve(src, step, k0):
        cres[...] = jnp.zeros_like(cres)

        @pl.loop(0, chunks)
        def _(c):
            wait_recv(fine(step, c))
            g = c // 2
            for i in range(CH):
                s = c * CH + i
                for j in range(slots):
                    for r0 in range(0, ny, RB):
                        rbuf[i, j, r0:r0 + RB] = dg[j, r0:r0 + RB] * change(
                            src, step, s, j, r0, weights(j, r0), -OMEGA)
                sums = [rows4(lambda k, j=j: rbuf[i, j, every4(k), :]) for j in range(slots)]
                cres[g] = cres[g] + dot(jnp.concatenate(sums, axis=0), qm[(c % 2) * CH + i])

        for g in range(2):
            first = cwb[...] * cres[g]
            for j in range(slots):
                cbs[g, j] = first[j * cy:(j + 1) * cy]
        for t in range(4):
            here = cbs if t == 0 else ce.at[t - 1]
            for g in range(2):
                csup[k0 + t, g] = here[g, top]
                csdn[k0 + t, g] = here[g, 0]
            start(coarse(k0 + t))
            if t < 3:
                wait_recv(coarse(k0 + t))
                for g in range(2):
                    for j in range(slots):
                        e = here[g, j]
                        lo = chlo[k0 + t, g] if j == 0 else here[g, j - 1]
                        above = jnp.zeros_like(e) if j == slots - 1 else here[g, j + 1]
                        hi = jnp.where(n - 1 == j, chhi[k0 + t, g], above)
                        ce[t, g, j] = (
                            cbs[g, j] + (1.0 - OMEGA) * e + cw[0, j] * lo + cw[1, j] * hi
                            + cw[2, j] * pltpu.roll(e, 1, 0) + cw[3, j] * pltpu.roll(e, cy - 1, 0)
                            + cw[4, j] * pltpu.roll(e, 1, 1) + cw[5, j] * pltpu.roll(e, nz - 1, 1))
        last = ce.at[2]
        wait_recv(coarse(k0 + 3))

        def add_correction(c):
            g = c // 2
            packed = jnp.concatenate(
                [last[g, j] for j in range(slots)] + [chlo[k0 + 3, g], chhi[k0 + 3, g]], axis=0)
            for i in range(CH):
                s = c * CH + i
                wide = dot(packed, qt[(c % 2) * CH + i])
                for k in range(4):
                    for j in range(slots):
                        at = pl.ds(PAD + k, cy, stride=4)
                        src[s, j, at, :] = src[s, j, at, :] + wide[j * cy:(j + 1) * cy]
                    at = every4(k)
                    hlo[step, s, at, :] = hlo[step, s, at, :] + wide[slots * cy:(slots + 1) * cy]
                    hhi[step, s, at, :] = hhi[step, s, at, :] + wide[(slots + 1) * cy:]

        return add_correction

    sweep(bs, va, PAD, 0)
    start(fwd_pair)
    correct = coarse_solve(va, 1, 0)
    sweep(va, vb, PAD, 1, correct)
    sweep(vb, va, PAD, 2)
    sweep(va, vb, PAD, 3)
    sweep(vb, va, PAD, 4)
    correct = coarse_solve(va, 5, 4)
    sweep(va, vb, PAD, 5, correct)
    sweep(vb, adj, 0, 6)

    zero = jnp.zeros_like(sy)
    sy[...] = zero
    sz[...] = zero
    sfa[...] = zero
    sx[...] = zero

    @pl.loop(0, nsrc)
    def _(s):
        for j in range(slots):
            f, a = fwd[s, j], adj[s, j]
            sfa[j] = sfa[j] + f * a
            sy[j] = sy[j] + ((f - jnp.where(row == 0, 0.0, pltpu.roll(f, 1, 0)))
                             * (a - jnp.where(row == 0, 0.0, pltpu.roll(a, 1, 0))))
            sz[j] = sz[j] + ((f - jnp.where(lane == 0, 0.0, pltpu.roll(f, 1, 1)))
                             * (a - jnp.where(lane == 0, 0.0, pltpu.roll(a, 1, 1))))
            if j > 0:
                sx[j] = sx[j] + (f - fwd[s, j - 1]) * (a - adj[s, j - 1])

    wait_recv(fwd_pair)
    for c in range(chunks):
        wait_recv(fine(STEPS - 1, c), up=c < chunks // 2, dn=c >= chunks // 2)
    lower, upper = plane, plane
    for s in range(half):
        lower = lower + (fwd[s, 0] - fhlo[s]) * (adj[s, 0] - hlo[STEPS - 1, s])
    plo[...] = lower
    for s in range(half):
        upper = upper + ((fwd[half + s, top] - fhhi[s])
                         * (adj[half + s, top] - hhi[STEPS - 1, half + s]))
    phi[...] = upper
    start(prod_pair)

    @pl.when(jnp.logical_not(has_lo))
    def _():
        total = plane
        for s in range(half, nsrc):
            total = total + fwd[s, 0] * adj[s, 0]
        rlo[...] = total

    @pl.when(jnp.logical_not(has_hi))
    def _():
        total = plane
        for s in range(half):
            total = total + fwd[s, top] * adj[s, top]
        rhi[...] = total

    for j in range(slots):
        y_hi = jnp.where(row == ny - 1, sfa[j], pltpu.roll(sy[j], ny - 1, 0))
        z_hi = jnp.where(lane == nz - 1, sfa[j], pltpu.roll(sz[j], nz - 1, 1))
        sy[j] = sy[j] + y_hi + sz[j] + z_hi
    wait_recv(prod_pair)
    for j in range(slots):
        x_lo = plo[...] + rlo[...] if j == 0 else sx[j]
        x_hi = jnp.where(n - 1 == j, phi[...] + rhi[...], plane if j == slots - 1 else sx[j + 1])
        grad[j] = jnp.where(j < n, -0.5, 0.0) * (sy[j] + x_lo + x_hi)

    @pl.loop(0, STEPS - 1)
    def _(k):
        for c in range(chunks):
            wait_send(fine(k, c))
    for c in range(chunks):
        wait_send(fine(STEPS - 1, c), up=c < chunks // 2, dn=c >= chunks // 2)

    @pl.loop(0, CSTEPS)
    def _(k):
        wait_send(coarse(k))
    for pair in (cond_pair, fwd_pair, prod_pair):
        wait_send(pair)


def shards(conductivity, forward, adjoint_rhs, plane_counts):
    slots, ny, nz = conductivity.shape
    nsrc = forward.shape[0]
    half, chunks, cy = nsrc // 2, nsrc // CH, ny // 4
    n = lax.dynamic_slice(plane_counts, (lax.axis_index("space"),), (1,))
    vmem = functools.partial(pl.BlockSpec, memory_space=pltpu.VMEM)

    def buf(*shape):
        return pltpu.VMEM(shape, F32)

    def sems(*shape):
        return pltpu.SemaphoreType.DMA(shape)

    field = (nsrc, slots, ny + 2 * PAD, nz)
    scratch = [
        buf(7, slots, ny, nz), buf(slots, ny, nz), buf(*field), buf(*field), buf(*field),
        *[buf(STEPS, nsrc, ny, nz)] * 4,
        *[buf(half, ny, nz)] * 4,
        buf(4, nz, nz), buf(4, nz, nz),
        buf(6, slots, cy, nz), buf(slots * cy, nz), buf(2, slots * cy, nz),
        buf(2, slots, cy, nz), buf(3, 2, slots, cy, nz),
        *[buf(CSTEPS, 2, cy, nz)] * 4,
        *[buf(ny, nz)] * 8,
        *[buf(slots, ny, nz)] * 4,
        buf(CH, slots, ny, nz),
        *[sems(STEPS, chunks)] * 4,
        *[sems(CSTEPS)] * 4,
        *[sems(3)] * 4,
    ]
    return pl.pallas_call(
        kernel,
        out_shape=(jax.ShapeDtypeStruct(forward.shape, F32),
                   jax.ShapeDtypeStruct(conductivity.shape, F32)),
        in_specs=[pl.BlockSpec(memory_space=pltpu.SMEM), vmem(), vmem(), vmem()],
        out_specs=(vmem(), vmem()),
        scratch_shapes=scratch,
        compiler_params=pltpu.CompilerParams(
            collective_id=0, has_side_effects=True, vmem_limit_bytes=56 * 2**20),
    )(n, conductivity, forward, adjoint_rhs)


def solution(mesh):
    in_specs = (
        P("space", "groups", None),
        P("groups", "space", None, None),
        P("groups", "space", None, None),
        P("groups"),
    )
    out_specs = (P("groups", "space", None, None), P("space", "groups", None))
    return jax.shard_map(shards, mesh=mesh, in_specs=in_specs, out_specs=out_specs, check_vma=False)
```

time: 505 us -> 138 us (0.27); the launches traced: 495 us -> 137 us
  Pallas kernels: 0 us -> 132 us
  local copies, waits for them, and re-layouts: 137 us -> 5.13 us
  other arithmetic: 125 us -> 0 us
  waiting for transfers between devices: 121 us -> 0 us
  starting transfers between devices: 109 us -> 0 us
    pallas_call x0 -> x1, Pallas kernels: none -> 132 us  [shards(): pl.pallas_call(kernel, out_shape=(jax.ShapeDtypeStruct(forward.shape, F32...]
    ppermute x38 -> x0, waiting for transfers between devices: 121 us -> none  [the longest x19 115 us: extended_2(): after = lax.ppermute(leading, axis, down)]
    ppermute x38 -> x0, starting transfers between devices: 109 us -> none  [the longest x19 66.6 us: extended_2(): before = lax.ppermute(last, axis, up)]
    select_n x19 -> x0, other arithmetic: 77.4 us -> none  [the longest x8 44.8 us: shards(): correction = jnp.where(alive_mask, coarse_updated, 0.0)]
    select_n x4 -> x0, local copies, waits for them, and re-layouts: 58.5 us -> none  [the longest x2 52.5 us: shards(): residue = jnp.where(alive_mask, residue, 0.0)]
    reduce_sum x6 -> x0, other arithmetic: 41.7 us -> none  [the longest x2 28.8 us: block_sum(): values.reshape(shape[0], shape[1], shape[2] // 4, 4, shape[3] // 4, 4)]
    slice x39 -> x0, local copies, waits for them, and re-layouts: 21.7 us -> none  [the longest x13 8.35 us: slab_neighbors(): lower_side = jnp.concatenate([lower_plane[:, None], values[:, :-1]], axis=1)]
    another operation x5 -> x0, local copies, waits for them, and re-layouts: 17.3 us -> none  [the longest x3 17 us: block_mean(): values.reshape(shape[0], shape[1], shape[2] // 4, 4, shape[3] // 4, 4)]
  transfers between devices with their start and end apart: 38 -> 0, of which waited for: 16 -> 0; matrix products, arithmetic and copies ran while one was open for 24% -> 0% of each run, Pallas kernels for 0% -> 0%
where the time goes in v1:
time: 138 us; the launch traced here: 137 us
  Pallas kernels  132 us (96%)
  local copies, waits for them, and re-layouts  5.13 us (4%)
    pallas_call x1, Pallas kernels, shards(): pl.pallas_call(kernel, out_shape=(jax.ShapeDtypeStruct(forward.shape, F32...  132 us
    unnamed x4, local copies, waits for them, and re-layouts  3.88 us

profile of v1, /device:TPU:17, one launch (start us, length us, event | category | flops | bytes accessed | tf_op | source)
XLA Modules:
  0.0 137.4 jit_solution(7205893791145168962)
XLA Ops:
  0.6 1.2 dynamic_slice.3.n_ref
  1.9 131.7 %shard_map.59 = (f32[8,4,128,128]{3,2,1,0:T(8,128)}, f32[4,128,128]{2,1,0:T(8,128)}) custom-call(s32[1]{0:T(128)} %dynamic_slice.3.n_ref, f32[4,128,128]{2,1,0:T(8,128)} %cond.1, f32[8,4,128,128]{3,2,1,0:T(8,128)} %fwd.1, f32[8,4,128,128]{3,2,1,0:T(8,128)} %rhs.1), custom_call_target="tpu_custom_call" | custom-call | tf_op jit(solution)/shard_map/pallas_call | solution.py:439
  133.6 0.0 copy-start
  133.6 3.2 %copy.8 = f32[8,4,128,128]{3,2,1,0:T(8,128)} copy(f32[8,4,128,128]{3,2,1,0:T(8,128)} %get-tuple-element.4) | data formatting | bytes 4194304
  136.7 0.0 copy-done
  136.7 0.7 copy.9
Async XLA Ops:
  133.6 3.2 %copy-start = (f32[4,128,128]{2,1,0:T(8,128)S(1)}, f32[4,128,128]{2,1,0:T(8,128)}, u32[]{:S(2)}) copy-start(f32[4,128,128]{2,1,0:T(8,128)} %get-tuple-element.5) | copy-start | bytes 786436

commit v2 on v1

--- a/solution.py
+++ b/solution.py
@@ -13,7 +13,7 @@
 RB = 32
 CH = 2
 STEPS = 8
-CSTEPS = 8
+CSTEPS = 10
 
 
 def dot(a, b):
@@ -23,7 +23,7 @@
 def kernel(n_ref, cond, fwd, rhs, adj, grad,
            w, dg, bs, va, vb, hlo, hhi, sup, sdn, fhlo, fhhi, fsup, fsdn,
            qm, qt, cw, cwb, cres, cbs, ce, chlo, chhi, csup, csdn,
-           kup, kdn, klo, khi, plo, phi, rlo, rhi, sy, sz, sfa, sx, rbuf,
+           kup, kdn, klo, khi, plo, phi, rlo, rhi, sy, sz, sfa, sx, rbuf, fx, ebuf,
            up_send, up_recv, dn_send, dn_recv, cup_send, cup_recv, cdn_send, cdn_recv,
            mup_send, mup_recv, mdn_send, mdn_recv):
     slots, ny, nz = cond.shape
@@ -33,7 +33,7 @@
     cy = ny // 4
     pos = lax.axis_index("space")
     peers = lax.axis_size("space")
-    n = n_ref[0]
+    n = n_ref[pos]
     top = jnp.maximum(n - 1, 0)
     has_lo = pos > 0
     has_hi = pos < peers - 1
@@ -157,6 +157,8 @@
         fsdn[s] = fwd[half + s, 0]
 
     wait_recv(cond_pair)
+    fx[0] = (cond[top] + khi[...]) * 0.5
+    fx[1] = (cond[0] + klo[...]) * 0.5
 
     for j in range(slots):
         c = cond[j]
@@ -228,8 +230,12 @@
         o = PAD + r0
         rows = slice(o, o + RB)
         v = src[s, j, rows]
-        lo = hlo[step, s, r0:r0 + RB] if j == 0 else src[s, j - 1, rows]
-        edge_hi = hhi[step, s, r0:r0 + RB]
+        nothing = jnp.zeros_like(v)
+        if j > 0:
+            lo = src[s, j - 1, rows]
+        else:
+            lo = nothing if step is None else hlo[step, s, r0:r0 + RB]
+        edge_hi = nothing if step is None else hhi[step, s, r0:r0 + RB]
         above = jnp.zeros_like(edge_hi) if j == slots - 1 else src[s, j + 1, rows]
         hi = jnp.where(n - 1 == j, edge_hi, above)
         acc = bs[s, j, rows] + keep * v
@@ -240,7 +246,7 @@
     def weights(j, r0):
         return [w[i, j, r0:r0 + RB] for i in range(6)]
 
-    def sweep(src, dst, off, step, prepare=None):
+    def sweep(src, dst, off, step, prepare=None, ahead=chunks):
         @pl.loop(0, chunks)
         def _(c):
             if prepare is None:
@@ -257,7 +263,9 @@
             for i in range(CH):
                 stage(step + 1, c * CH + i, dst, off)
             if step + 1 < STEPS - 1:
-                start(fine(step + 1, c))
+                @pl.when(c < ahead)
+                def _():
+                    start(fine(step + 1, c))
             else:
                 first = c < chunks // 2
 
@@ -269,51 +277,70 @@
                 def _():
                     start(fine(step + 1, c), up=False)
 
-    def coarse_solve(src, step, k0):
+    def coarse_solve(src, step, k0, extra=None):
         cres[...] = jnp.zeros_like(cres)
+        csup[k0] = jnp.zeros(csup.shape[1:], F32)
+        csdn[k0] = jnp.zeros(csdn.shape[1:], F32)
 
         @pl.loop(0, chunks)
         def _(c):
-            wait_recv(fine(step, c))
             g = c // 2
             for i in range(CH):
                 s = c * CH + i
                 for j in range(slots):
                     for r0 in range(0, ny, RB):
                         rbuf[i, j, r0:r0 + RB] = dg[j, r0:r0 + RB] * change(
-                            src, step, s, j, r0, weights(j, r0), -OMEGA)
+                            src, None, s, j, r0, weights(j, r0), -OMEGA)
+                ebuf[i, 0] = fx[0] * sup[step, s]
+                ebuf[i, 1] = fx[1] * sdn[step, s]
                 sums = [rows4(lambda k, j=j: rbuf[i, j, every4(k), :]) for j in range(slots)]
-                cres[g] = cres[g] + dot(jnp.concatenate(sums, axis=0), qm[(c % 2) * CH + i])
+                sums += [rows4(lambda k, e=e: ebuf[i, e, every4(k), :]) for e in range(2)]
+                packed = dot(jnp.concatenate(sums, axis=0), qm[(c % 2) * CH + i])
+                cres[g] = cres[g] + packed[:slots * cy]
+                csup[k0, g] = csup[k0, g] + packed[slots * cy:(slots + 1) * cy]
+                csdn[k0, g] = csdn[k0, g] + packed[(slots + 1) * cy:]
+
+        start(coarse(k0))
+        start(fine(step, 1))
+        wait_recv(coarse(k0))
 
         for g in range(2):
-            first = cwb[...] * cres[g]
             for j in range(slots):
-                cbs[g, j] = first[j * cy:(j + 1) * cy]
+                part = slice(j * cy, (j + 1) * cy)
+                total = cres[g, part] + jnp.where(n - 1 == j, chhi[k0, g], 0.0)
+                if j == 0:
+                    total = total + chlo[k0, g]
+                cbs[g, j] = cwb[part] * total
         for t in range(4):
             here = cbs if t == 0 else ce.at[t - 1]
             for g in range(2):
-                csup[k0 + t, g] = here[g, top]
-                csdn[k0 + t, g] = here[g, 0]
-            start(coarse(k0 + t))
+                csup[k0 + 1 + t, g] = here[g, top]
+                csdn[k0 + 1 + t, g] = here[g, 0]
+            start(coarse(k0 + 1 + t))
+            if t + 2 < chunks:
+                start(fine(step, t + 2))
+            elif t == 2 and extra is not None:
+                start(extra)
             if t < 3:
-                wait_recv(coarse(k0 + t))
+                wait_recv(coarse(k0 + 1 + t))
                 for g in range(2):
                     for j in range(slots):
                         e = here[g, j]
-                        lo = chlo[k0 + t, g] if j == 0 else here[g, j - 1]
+                        lo = chlo[k0 + 1 + t, g] if j == 0 else here[g, j - 1]
                         above = jnp.zeros_like(e) if j == slots - 1 else here[g, j + 1]
-                        hi = jnp.where(n - 1 == j, chhi[k0 + t, g], above)
+                        hi = jnp.where(n - 1 == j, chhi[k0 + 1 + t, g], above)
                         ce[t, g, j] = (
                             cbs[g, j] + (1.0 - OMEGA) * e + cw[0, j] * lo + cw[1, j] * hi
                             + cw[2, j] * pltpu.roll(e, 1, 0) + cw[3, j] * pltpu.roll(e, cy - 1, 0)
                             + cw[4, j] * pltpu.roll(e, 1, 1) + cw[5, j] * pltpu.roll(e, nz - 1, 1))
         last = ce.at[2]
-        wait_recv(coarse(k0 + 3))
+        wait_recv(coarse(k0 + 4))
 
         def add_correction(c):
+            wait_recv(fine(step, c))
             g = c // 2
             packed = jnp.concatenate(
-                [last[g, j] for j in range(slots)] + [chlo[k0 + 3, g], chhi[k0 + 3, g]], axis=0)
+                [last[g, j] for j in range(slots)] + [chlo[k0 + 4, g], chhi[k0 + 4, g]], axis=0)
             for i in range(CH):
                 s = c * CH + i
                 wide = dot(packed, qt[(c % 2) * CH + i])
@@ -327,14 +354,13 @@
 
         return add_correction
 
-    sweep(bs, va, PAD, 0)
-    start(fwd_pair)
-    correct = coarse_solve(va, 1, 0)
+    sweep(bs, va, PAD, 0, ahead=1)
+    correct = coarse_solve(va, 1, 0, fwd_pair)
     sweep(va, vb, PAD, 1, correct)
     sweep(vb, va, PAD, 2)
     sweep(va, vb, PAD, 3)
-    sweep(vb, va, PAD, 4)
-    correct = coarse_solve(va, 5, 4)
+    sweep(vb, va, PAD, 4, ahead=1)
+    correct = coarse_solve(va, 5, 5)
     sweep(va, vb, PAD, 5, correct)
     sweep(vb, adj, 0, 6)
 
@@ -411,7 +437,6 @@
     slots, ny, nz = conductivity.shape
     nsrc = forward.shape[0]
     half, chunks, cy = nsrc // 2, nsrc // CH, ny // 4
-    n = lax.dynamic_slice(plane_counts, (lax.axis_index("space"),), (1,))
     vmem = functools.partial(pl.BlockSpec, memory_space=pltpu.VMEM)
 
     def buf(*shape):
@@ -431,7 +456,7 @@
         *[buf(CSTEPS, 2, cy, nz)] * 4,
         *[buf(ny, nz)] * 8,
         *[buf(slots, ny, nz)] * 4,
-        buf(CH, slots, ny, nz),
+        buf(CH, slots, ny, nz), buf(2, ny, nz), buf(CH, 2, ny, nz),
         *[sems(STEPS, chunks)] * 4,
         *[sems(CSTEPS)] * 4,
         *[sems(3)] * 4,
@@ -445,7 +470,7 @@
         scratch_shapes=scratch,
         compiler_params=pltpu.CompilerParams(
             collective_id=0, has_side_effects=True, vmem_limit_bytes=56 * 2**20),
-    )(n, conductivity, forward, adjoint_rhs)
+    )(plane_counts, conductivity, forward, adjoint_rhs)
 
 
 def solution(mesh):

time: 138 us -> 131 us (0.949)
  Pallas kernels: 132 us -> 126 us
    pallas_call x1, Pallas kernels: 132 us -> 126 us  [shards(): pl.pallas_call(kernel, out_shape=(jax.ShapeDtypeStruct(forward.shape, F32...]
where the time goes in v2:
time: 131 us; the launch traced here: 130 us
  Pallas kernels  126 us (96%)
  local copies, waits for them, and re-layouts  3.88 us (3%)
    pallas_call x1, Pallas kernels, shards(): pl.pallas_call(kernel, out_shape=(jax.ShapeDtypeStruct(forward.shape, F32...  126 us
    unnamed x4, local copies, waits for them, and re-layouts  3.88 us

profile of v2, /device:TPU:17, one launch (start us, length us, event | category | flops | bytes accessed | tf_op | source)
XLA Modules:
  0.0 130.3 jit_solution(13071104553185107271)
XLA Ops:
  0.6 125.8 %shard_map.59 = (f32[8,4,128,128]{3,2,1,0:T(8,128)}, f32[4,128,128]{2,1,0:T(8,128)}) custom-call(s32[16]{0:T(128)} %n_ref.1, f32[4,128,128]{2,1,0:T(8,128)} %cond.1, f32[8,4,128,128]{3,2,1,0:T(8,128)} %fwd.1, f32[8,4,128,128]{3,2,1,0:T(8,128)} %rhs.1), custom_call_target="tpu_custom_call" | custom-call | tf_op jit(solution)/shard_map/pallas_call | solution.py:464
  126.4 0.0 copy-start
  126.4 3.2 %copy.8 = f32[8,4,128,128]{3,2,1,0:T(8,128)} copy(f32[8,4,128,128]{3,2,1,0:T(8,128)} %get-tuple-element.4) | data formatting | bytes 4194304
  129.6 0.0 copy-done
  129.6 0.7 copy.9
Async XLA Ops:
  126.4 3.2 %copy-start = (f32[4,128,128]{2,1,0:T(8,128)S(1)}, f32[4,128,128]{2,1,0:T(8,128)}, u32[]{:S(2)}) copy-start(f32[4,128,128]{2,1,0:T(8,128)} %get-tuple-element.5) | copy-start | bytes 786436

commit v3 on v2

--- a/solution.py
+++ b/solution.py
@@ -23,7 +23,7 @@
 def kernel(n_ref, cond, fwd, rhs, adj, grad,
            w, dg, bs, va, vb, hlo, hhi, sup, sdn, fhlo, fhhi, fsup, fsdn,
            qm, qt, cw, cwb, cres, cbs, ce, chlo, chhi, csup, csdn,
-           kup, kdn, klo, khi, plo, phi, rlo, rhi, sy, sz, sfa, sx, rbuf, fx, ebuf,
+           kup, kdn, klo, khi, wup, wdn, wlo, whi, plo, phi, rlo, rhi, sy, sz, sfa, sx, rbuf, fx, ebuf,
            up_send, up_recv, dn_send, dn_recv, cup_send, cup_recv, cdn_send, cdn_recv,
            mup_send, mup_recv, mdn_send, mdn_recv):
     slots, ny, nz = cond.shape
@@ -79,6 +79,7 @@
 
     cond_pair = misc(0, kup, klo, kdn, khi)
     fwd_pair = misc(1, fsup, fhlo, fsdn, fhhi)
+    scale_pair = misc(3, wup, wlo, wdn, whi)
     prod_pair = misc(2, phi, rlo, plo, rhi)
 
     def start(pair, up=True, dn=True):
@@ -115,11 +116,19 @@
     kdn[...] = cond[0]
     start(cond_pair)
 
+    for c in range(chunks):
+        for i in range(CH):
+            sup[0, c * CH + i] = rhs[c * CH + i, top]
+            sdn[0, c * CH + i] = rhs[c * CH + i, 0]
+        if c < chunks // 2:
+            start(fine(0, c))
+
     plane = jnp.zeros((ny, nz), F32)
 
     @pl.when(jnp.logical_not(has_lo))
     def _():
         klo[...] = plane
+        wlo[...] = plane
         chlo[...] = jnp.zeros_like(chlo)
         fhlo[...] = jnp.zeros_like(fhlo)
 
@@ -130,6 +139,7 @@
     @pl.when(jnp.logical_not(has_hi))
     def _():
         khi[...] = plane
+        whi[...] = plane
         chhi[...] = jnp.zeros_like(chhi)
         fhhi[...] = jnp.zeros_like(fhhi)
 
@@ -184,14 +194,18 @@
         sup[step, s] = buf[s, top, off:off + ny]
         sdn[step, s] = buf[s, 0, off:off + ny]
 
+    wup[...] = w[6, top]
+    wdn[...] = w[6, 0]
+    start(scale_pair)
+    for c in range(chunks // 2, chunks):
+        start(fine(0, c))
+
     @pl.loop(0, chunks)
     def _(c):
         for i in range(CH):
             s = c * CH + i
             for j in range(slots):
                 bs[s, j, PAD:PAD + ny] = w[6, j] * rhs[s, j]
-            stage(0, s, bs, PAD)
-        start(fine(0, c))
 
     qall = jnp.where(row // 4 == lane % 32, 1.0 / 16.0, 0.0).astype(F32)
 
@@ -354,7 +368,16 @@
 
         return add_correction
 
-    sweep(bs, va, PAD, 0, ahead=1)
+    wait_recv(scale_pair)
+
+    def scale_planes(c):
+        wait_recv(fine(0, c))
+        for i in range(CH):
+            s = c * CH + i
+            hlo[0, s] = hlo[0, s] * wlo[...]
+            hhi[0, s] = hhi[0, s] * whi[...]
+
+    sweep(bs, va, PAD, 0, scale_planes, ahead=1)
     correct = coarse_solve(va, 1, 0, fwd_pair)
     sweep(va, vb, PAD, 1, correct)
     sweep(vb, va, PAD, 2)
@@ -429,7 +452,7 @@
     @pl.loop(0, CSTEPS)
     def _(k):
         wait_send(coarse(k))
-    for pair in (cond_pair, fwd_pair, prod_pair):
+    for pair in (cond_pair, fwd_pair, prod_pair, scale_pair):
         wait_send(pair)
 
 
@@ -454,12 +477,12 @@
         buf(6, slots, cy, nz), buf(slots * cy, nz), buf(2, slots * cy, nz),
         buf(2, slots, cy, nz), buf(3, 2, slots, cy, nz),
         *[buf(CSTEPS, 2, cy, nz)] * 4,
-        *[buf(ny, nz)] * 8,
+        *[buf(ny, nz)] * 12,
         *[buf(slots, ny, nz)] * 4,
         buf(CH, slots, ny, nz), buf(2, ny, nz), buf(CH, 2, ny, nz),
         *[sems(STEPS, chunks)] * 4,
         *[sems(CSTEPS)] * 4,
-        *[sems(3)] * 4,
+        *[sems(4)] * 4,
     ]
     return pl.pallas_call(
         kernel,

time: 131 us -> 133 us (1.015)
  Pallas kernels: 126 us -> 128 us
    pallas_call x1, Pallas kernels: 126 us -> 128 us  [shards(): pl.pallas_call(kernel, out_shape=(jax.ShapeDtypeStruct(forward.shape, F32...]
where the time goes in v3:
time: 133 us
  Pallas kernels  128 us (96%)
  local copies, waits for them, and re-layouts  3.88 us (3%)
    pallas_call x1, Pallas kernels, shards(): pl.pallas_call(kernel, out_shape=(jax.ShapeDtypeStruct(forward.shape, F32...  128 us
    unnamed x4, local copies, waits for them, and re-layouts  3.88 us

profile of v3, /device:TPU:17, one launch (start us, length us, event | category | flops | bytes accessed | tf_op | source)
XLA Modules:
  0.0 132.6 jit_solution(11717527114873462418)
XLA Ops:
  0.6 128.1 %shard_map.59 = (f32[8,4,128,128]{3,2,1,0:T(8,128)}, f32[4,128,128]{2,1,0:T(8,128)}) custom-call(s32[16]{0:T(128)} %n_ref.1, f32[4,128,128]{2,1,0:T(8,128)} %cond.1, f32[8,4,128,128]{3,2,1,0:T(8,128)} %fwd.1, f32[8,4,128,128]{3,2,1,0:T(8,128)} %rhs.1), custom_call_target="tpu_custom_call" | custom-call | tf_op jit(solution)/shard_map/pallas_call | solution.py:487
  128.7 0.0 copy-start
  128.7 3.2 %copy.8 = f32[8,4,128,128]{3,2,1,0:T(8,128)} copy(f32[8,4,128,128]{3,2,1,0:T(8,128)} %get-tuple-element.4) | data formatting | bytes 4194304
  131.9 0.0 copy-done
  131.9 0.7 copy.9
Async XLA Ops:
  128.7 3.2 %copy-start = (f32[4,128,128]{2,1,0:T(8,128)S(1)}, f32[4,128,128]{2,1,0:T(8,128)}, u32[]{:S(2)}) copy-start(f32[4,128,128]{2,1,0:T(8,128)} %get-tuple-element.5) | copy-start | bytes 786436
